TPU v7x, 256 devices: a whole 4x4x8 slice. The times are simulated.
256 devices in a mesh: leaf: 64 (over y, x, z_hi), head: 4 (over z_lo, core).
Axes of the slice: x: 4, y: 4, z: 8 (z_hi: 4, z_lo: 2; z = z_hi * 2 + z_lo), core: 2. Of those that a mesh axis runs over, the one named last changes fastest.
Arguments:
- root_query: bfloat16 [1024, 8192], P('leaf', 'head'), may hold values from -6 to 6
- branch_query: bfloat16 [4096, 8192], P('leaf', 'head'), may hold values from -6 to 6
- leaf_query: bfloat16 [8192, 8192], P('leaf', 'head'), may hold values from -8 to 8
- root_key: bfloat16 [1024, 1024], P(('leaf', 'head')), may hold values from -6 to 6
- root_value: bfloat16 [1024, 1024], P(('leaf', 'head')), may hold values from -6 to 6
- branch_key: bfloat16 [4096, 1024], P('leaf', 'head'), may hold values from -6 to 6
- branch_value: bfloat16 [4096, 1024], P('leaf', 'head'), may hold values from -6 to 6
- leaf_key: bfloat16 [8192, 1024], P('leaf', 'head'), may hold values from -8 to 8
- leaf_value: bfloat16 [8192, 1024], P('leaf', 'head'), may hold values from -6 to 6
- root_grad_out: bfloat16 [1024, 8192], P('leaf', 'head'), may hold values from -6 to 6
- branch_grad_out: bfloat16 [4096, 8192], P('leaf', 'head'), may hold values from -6 to 6
- leaf_grad_out: bfloat16 [8192, 8192], P('leaf', 'head'), may hold values from -6 to 6
- branch_lengths: int32 [8], replicated, may hold values from 1 to 512, 2901 in all
- leaf_lengths: int32 [64], P('leaf'), may hold values from 1 to 128, 5504 in all
Outputs:
- root_attended: bfloat16 [1024, 8192], P('leaf', 'head')
- branch_attended: bfloat16 [4096, 8192], P('leaf', 'head')
- leaf_attended: bfloat16 [8192, 8192], P('leaf', 'head')
- root_query_grad: bfloat16 [1024, 8192], P('leaf', 'head')
- branch_query_grad: bfloat16 [4096, 8192], P('leaf', 'head')
- leaf_query_grad: bfloat16 [8192, 8192], P('leaf', 'head')
- root_key_grad: bfloat16 [1024, 1024], P(('leaf', 'head'))
- root_value_grad: bfloat16 [1024, 1024], P(('leaf', 'head'))
- branch_key_grad: bfloat16 [4096, 1024], P('leaf', 'head')
- branch_value_grad: bfloat16 [4096, 1024], P('leaf', 'head')
- leaf_key_grad: bfloat16 [8192, 1024], P('leaf', 'head')
- leaf_value_grad: bfloat16 [8192, 1024], P('leaf', 'head')
Inputs may be any that keep to these rules, and one draw needn't show every extreme that they name: `branch_lengths`: some branch has all 512 tokens live. `leaf_lengths`: some leaf has all 128 tokens live.
All inputs are finite; a program needn't handle non-finite values. No bound on the sum of `leaf_lengths` on one device may be relied on, other than what follows from the above.
Results may differ from a plain program's by a relative error of at most 0.013.
Values may be sent and summed in bfloat16 or wider, within the bound.
No kernel may reach another device: no remote copies, remote signals or barrier semaphores. Data moves between devices by JAX's collectives and lax.ppermute only.
A program may use at most 128 MiB of HBM per device.

v0:
```python
import math

import jax
import jax.numpy as jnp
from jax import lax
from jax.sharding import PartitionSpec as P

HEAD_DIM = 128
GROUP = 8


def tree_mask(
    root_place, branch_place, branch_live, leaf_live, root_count, branch_count, leaf_count
):
    query_kind = jnp.concatenate(
        [
            jnp.zeros(root_place.shape, jnp.int32),
            jnp.ones(branch_place.shape, jnp.int32),
            jnp.full((leaf_count,), 2, jnp.int32),
        ]
    )
    query_place = jnp.concatenate(
        [root_place, branch_place, jnp.arange(leaf_count, dtype=jnp.int32)]
    )
    key_kind = jnp.concatenate(
        [
            jnp.zeros((root_count,), jnp.int32),
            jnp.ones((branch_count,), jnp.int32),
            jnp.full((leaf_count,), 2, jnp.int32),
        ]
    )
    key_place = jnp.concatenate(
        [
            jnp.arange(root_count, dtype=jnp.int32),
            jnp.arange(branch_count, dtype=jnp.int32),
            jnp.arange(leaf_count, dtype=jnp.int32),
        ]
    )
    row_kind = query_kind[:, None]
    row_place = query_place[:, None]
    col_kind = key_kind[None, :]
    col_place = key_place[None, :]
    causal = col_place <= row_place
    from_root = (col_kind == 0) & ((row_kind > 0) | causal)
    from_branch = (
        (col_kind == 1) & (row_kind > 0) & (col_place < branch_live) & ((row_kind == 2) | causal)
    )
    from_leaf = (col_kind == 2) & (row_kind == 2) & (col_place < leaf_live) & causal
    allowed = from_root | from_branch | from_leaf
    live = (
        (query_kind == 0)
        | (query_kind == 1) & (query_place < branch_live)
        | (query_kind == 2) & (query_place < leaf_live)
    )
    return (allowed, live)


def group_terms(query, key, value, grad, allowed):
    scale = 1.0 / math.sqrt(query.shape[-1])
    scores = jnp.einsum("qgd,nd->gqn", query, key, preferred_element_type=jnp.float32) * scale
    scores = jnp.where(allowed[None], scores, -jnp.inf)
    top = jnp.max(scores, axis=-1, keepdims=True)
    expo = jnp.exp(scores - top)
    weights = expo / jnp.sum(expo, axis=-1, keepdims=True)
    rounded = weights.astype(jnp.bfloat16)
    attended = jnp.einsum("gqn,nd->qgd", rounded, value, preferred_element_type=jnp.float32)
    weight_grad = jnp.einsum("qgd,nd->gqn", grad, value, preferred_element_type=jnp.float32)
    delta = jnp.sum(weights * weight_grad, axis=-1, keepdims=True)
    score_grad = (weights * (weight_grad - delta) * scale).astype(jnp.bfloat16)
    query_grad = jnp.einsum("gqn,nd->qgd", score_grad, key, preferred_element_type=jnp.float32)
    key_grad = jnp.einsum("gqn,qgd->nd", score_grad, query, preferred_element_type=jnp.float32)
    value_grad = jnp.einsum("gqn,qgd->nd", rounded, grad, preferred_element_type=jnp.float32)
    return (attended, query_grad, key_grad, value_grad)


def all_heads(queries, keys, values, grads, allowed, live):
    masked = jnp.where(live[:, None], grads, jnp.zeros_like(grads))
    live_rows = live.astype(jnp.float32)[:, None]
    kv_count = keys.shape[1] // HEAD_DIM
    per_group = queries.shape[1] // kv_count
    rows = queries.shape[0]
    outs_a, outs_q, outs_k, outs_v = ([], [], [], [])
    for index in range(kv_count):
        query = queries[:, index * per_group : (index + 1) * per_group].reshape(rows, -1, HEAD_DIM)
        grad = masked[:, index * per_group : (index + 1) * per_group].reshape(rows, -1, HEAD_DIM)
        key = keys[:, index * HEAD_DIM : (index + 1) * HEAD_DIM]
        value = values[:, index * HEAD_DIM : (index + 1) * HEAD_DIM]
        attended, query_grad, key_grad, value_grad = group_terms(query, key, value, grad, allowed)
        outs_a.append(attended.reshape(rows, per_group))
        outs_q.append(query_grad.reshape(rows, per_group))
        outs_k.append(key_grad)
        outs_v.append(value_grad)
    attended = (jnp.concatenate(outs_a, 1) * live_rows).astype(jnp.bfloat16)
    query_grad = jnp.concatenate(outs_q, 1).astype(jnp.bfloat16)
    return (attended, query_grad, jnp.concatenate(outs_k, 1), jnp.concatenate(outs_v, 1))


def split_gathered(gathered, leaf_count, root_share, branch_index):
    columns = gathered.shape[1]
    blocks = gathered.reshape(leaf_count, -1, columns)
    root_part = blocks[:, :root_share].reshape(-1, columns)
    own = lax.dynamic_slice_in_dim(blocks, branch_index * GROUP, GROUP, 0)[:, root_share:]
    return (root_part, own.reshape(-1, columns))


def owner_rows(root_terms, branch_terms, leaf_count, branch_index):
    columns = root_terms.shape[1]
    share = branch_terms.shape[0] // GROUP
    spread = jnp.zeros((leaf_count, share, columns), jnp.float32)
    spread = lax.dynamic_update_slice_in_dim(
        spread, branch_terms.reshape(GROUP, share, columns), branch_index * GROUP, 0
    )
    return jnp.concatenate([root_terms.reshape(leaf_count, -1, columns), spread], 1).reshape(
        -1, columns
    )


def local(
    root_query,
    branch_query,
    leaf_query,
    root_key,
    root_value,
    branch_key,
    branch_value,
    leaf_key,
    leaf_value,
    root_grad_out,
    branch_grad_out,
    leaf_grad_out,
    branch_lengths,
    leaf_lengths,
):
    leaf_index = lax.axis_index("leaf")
    leaf_count = lax.axis_size("leaf")
    branch_index = leaf_index // GROUP
    within = leaf_index % GROUP
    root_keys, root_values = (
        lax.all_to_all(root_key, "head", split_axis=1, concat_axis=0, tiled=True),
        lax.all_to_all(root_value, "head", split_axis=1, concat_axis=0, tiled=True),
    )
    root_share = root_keys.shape[0]
    branch_share = branch_key.shape[0]
    branch_total = branch_share * GROUP
    leaf_rows = leaf_key.shape[0]
    gathered_keys, gathered_values = (
        lax.all_gather(jnp.concatenate([root_keys, branch_key], 0), "leaf", axis=0, tiled=True),
        lax.all_gather(jnp.concatenate([root_values, branch_value], 0), "leaf", axis=0, tiled=True),
    )
    whole_root_keys, branch_keys = split_gathered(
        gathered_keys, leaf_count, root_share, branch_index
    )
    whole_root_values, branch_values = split_gathered(
        gathered_values, leaf_count, root_share, branch_index
    )
    root_total = whole_root_keys.shape[0]
    branch_live = jnp.sum(
        jnp.where(
            jnp.arange(branch_lengths.shape[0], dtype=jnp.int32) == branch_index, branch_lengths, 0
        )
    )
    leaf_live = leaf_lengths[0]
    root_place = leaf_index * root_share + jnp.arange(root_share, dtype=jnp.int32)
    branch_place = within * branch_share + jnp.arange(branch_share, dtype=jnp.int32)
    allowed, live = tree_mask(
        root_place, branch_place, branch_live, leaf_live, root_total, branch_total, leaf_rows
    )
    queries = jnp.concatenate([root_query, branch_query, leaf_query], 0)
    grads = jnp.concatenate([root_grad_out, branch_grad_out, leaf_grad_out], 0)
    keys = jnp.concatenate([whole_root_keys, branch_keys, leaf_key], 0)
    values = jnp.concatenate([whole_root_values, branch_values, leaf_value], 0)
    attended, query_grad, key_grad, value_grad = all_heads(
        queries, keys, values, grads, allowed, live
    )
    middle = root_share + branch_share
    branch_end = root_total + branch_total
    root_key_terms = key_grad[:root_total]
    root_value_terms = value_grad[:root_total]
    branch_key_terms = key_grad[root_total:branch_end]
    branch_value_terms = value_grad[root_total:branch_end]
    summed_keys, summed_values = (
        lax.psum_scatter(
            owner_rows(root_key_terms, branch_key_terms, leaf_count, branch_index),
            "leaf",
            scatter_dimension=0,
            tiled=True,
        ),
        lax.psum_scatter(
            owner_rows(root_value_terms, branch_value_terms, leaf_count, branch_index),
            "leaf",
            scatter_dimension=0,
            tiled=True,
        ),
    )
    root_key_sum = summed_keys[:root_share]
    root_value_sum = summed_values[:root_share]
    branch_key_sum = summed_keys[root_share:]
    branch_value_sum = summed_values[root_share:]
    root_key_grad, root_value_grad = (
        lax.all_to_all(
            root_key_sum.astype(jnp.bfloat16), "head", split_axis=0, concat_axis=1, tiled=True
        ),
        lax.all_to_all(
            root_value_sum.astype(jnp.bfloat16), "head", split_axis=0, concat_axis=1, tiled=True
        ),
    )
    return (
        attended[:root_share],
        attended[root_share:middle],
        attended[middle:],
        query_grad[:root_share],
        query_grad[root_share:middle],
        query_grad[middle:],
        root_key_grad,
        root_value_grad,
        branch_key_sum.astype(jnp.bfloat16),
        branch_value_sum.astype(jnp.bfloat16),
        key_grad[branch_end:].astype(jnp.bfloat16),
        value_grad[branch_end:].astype(jnp.bfloat16),
    )


def solution(mesh):
    return jax.shard_map(
        local,
        mesh=mesh,
        in_specs=(
            P("leaf", "head"),
            P("leaf", "head"),
            P("leaf", "head"),
            P(("leaf", "head"), None),
            P(("leaf", "head"), None),
            P("leaf", "head"),
            P("leaf", "head"),
            P("leaf", "head"),
            P("leaf", "head"),
            P("leaf", "head"),
            P("leaf", "head"),
            P("leaf", "head"),
            P(),
            P("leaf"),
        ),
        out_specs=(
            P("leaf", "head"),
            P("leaf", "head"),
            P("leaf", "head"),
            P("leaf", "head"),
            P("leaf", "head"),
            P("leaf", "head"),
            P(("leaf", "head"), None),
            P(("leaf", "head"), None),
            P("leaf", "head"),
            P("leaf", "head"),
            P("leaf", "head"),
            P("leaf", "head"),
        ),
        check_vma=False,
    )
```

profile of v0, /device:TPU:1, one launch (start us, length us, event | category | flops | bytes accessed | tf_op | source)
XLA Modules:
  0.0 1028.0 jit_solution(8454779505249648090)
XLA Ops:
  7.2 9.6 all_to_all.76
  18.3 7.0 all_to_all.77
  35.8 2.7 fusion.43
  38.5 61.1 %all-gather.5.cloned.1.call-done = bf16[5120,256]{1,0:T(8,128)(2,1)} async-done(((bf16[80,256]{1,0:T(8,128)(2,1)}), bf16[5120,256]{1,0:T(8,128)(2,1)}) %all-gather.5.cloned.1.call-update) | async-done | bytes 2621456 | tf_op jit(solution)/shard_map/all_gather | solution.py:147
  100.7 81.8 %all-gather.3.cloned.1.call-done = bf16[5120,256]{1,0:T(8,128)(2,1)} async-done(((bf16[80,256]{1,0:T(8,128)(2,1)}), bf16[5120,256]{1,0:T(8,128)(2,1)}) %all-gather.3.cloned.1.call-update) | async-done | bytes 2621456 | tf_op jit(solution)/shard_map/all_gather | solution.py:148
  185.2 8.0 fusion.120
  193.3 7.8 fusion.115
  201.1 5.4 fusion.32
  215.1 2.8 pad_maximum_fusion.1
  220.1 7.1 fusion.67
  227.2 22.9 %fusion.39 = f32[1664,128]{0,1:T(8,128)S(1)} fusion(f32[1664,208,8]{0,1,2:T(8,128)} %fusion.67, bf16[26,8,8,128]{3,2,1,0:T(8,128)(2,1)} %copy-done.6, f32[8,208,1664]{2,1,0:T(8,128)} %get-tuple-element.48, f32[8,208]{1,0:T(8,128)S(1)} %get-tuple-element.47), kind=kOutput, calls=%fused_computation.47 | convolution fusion | flops 728222976 | bytes 23435776 | tf_op jit(solution)/shard_map/gqn,qgd->nd/dot_general | solution.py:71
  250.1 6.6 fusion.64
  256.7 23.0 %fusion.38 = f32[1664,128]{0,1:T(8,128)S(1)} fusion(f32[1664,208,8]{0,1,2:T(8,128)} %fusion.64, bf16[26,8,8,128]{3,2,1,0:T(8,128)(2,1)} %copy-done.5, f32[8,208,1664]{2,1,0:T(8,128)} %get-tuple-element.46, f32[8,208]{1,0:T(8,128)S(1)} %get-tuple-element.45), kind=kOutput, calls=%fused_computation.46 | convolution fusion | flops 728222976 | bytes 23435776 | tf_op jit(solution)/shard_map/gqn,qgd->nd/dot_general | solution.py:71
  280.9 2.5 copy.48
  287.9 4.1 pad_maximum_fusion
  292.0 5.4 fusion.45
  298.5 5.2 fusion.48
  304.7 19.0 %fusion.57 = bf16[8,26,8,128]{3,2,1,0:T(8,128)(2,1)} fusion(f32[1664,208,8]{0,1,2:T(8,128)} %fusion.67, bf16[1664,256]{1,0:T(8,128)(2,1)} %copy-done.4, f32[8,208,1664]{2,1,0:T(8,128)} %get-tuple-element.48, f32[8,208]{1,0:T(8,128)S(1)} %get-tuple-element.47), kind=kOutput, calls=%fused_computation.71 | convolution fusion | flops 728435968 | bytes 45170688 | tf_op jit(solution)/shard_map/gqn,nd->qgd/dot_general | solution.py:70
  325.6 18.7 %fusion.58 = bf16[8,26,8,128]{3,2,1,0:T(8,128)(2,1)} fusion(f32[1664,208,8]{0,1,2:T(8,128)} %fusion.64, bf16[1664,256]{1,0:T(8,128)(2,1)} %copy-done.4, f32[8,208,1664]{2,1,0:T(8,128)} %get-tuple-element.46, f32[8,208]{1,0:T(8,128)S(1)} %get-tuple-element.45), kind=kOutput, calls=%fused_computation.72 | convolution fusion | flops 728435968 | bytes 45170688 | tf_op jit(solution)/shard_map/gqn,nd->qgd/dot_general | solution.py:70
  346.1 2.5 fusion.40
  348.6 215.2 %reduce-scatter.5.cloned.1.call-done = f32[80,256]{1,0:T(8,128)} async-done(((f32[5120,256]{1,0:T(8,128)}), f32[80,256]{1,0:T(8,128)}) %reduce-scatter.5.cloned.1.call-update) | async-done | bytes 81936 | tf_op jit(solution)/shard_map/reduce_scatter | solution.py:188
  565.3 51.9 %all-to-all-start.3 = ((bf16[4,4,256]{2,1,0:T(4,128)(2,1)}), bf16[4,4,256]{2,1,0:T(4,128)(2,1)S(1)}, u32[]{:S(2)}, u32[]{:S(2)}) async-start(bf16[4,4,256]{2,1,0:T(4,128)(2,1)} %all_to_all.68), calls=%async_computation.5 | async-start | bytes 16384 | tf_op jit(solution)/shard_map/all_to_all | solution.py:203
  617.2 334.4 %reduce-scatter.3.cloned.1.call-done = f32[80,256]{1,0:T(8,128)} async-done(((f32[5120,256]{1,0:T(8,128)}), f32[80,256]{1,0:T(8,128)}) %reduce-scatter.3.cloned.1.call-update) | async-done | bytes 81936 | tf_op jit(solution)/shard_map/reduce_scatter | solution.py:182
  953.1 54.4 %all-to-all-start.2 = ((bf16[4,4,256]{2,1,0:T(4,128)(2,1)}), bf16[4,4,256]{2,1,0:T(4,128)(2,1)S(1)}, u32[]{:S(2)}, u32[]{:S(2)}) async-start(bf16[4,4,256]{2,1,0:T(4,128)(2,1)} %all_to_all.64), calls=%async_computation.3 | async-start | bytes 16384 | tf_op jit(solution)/shard_map/all_to_all | solution.py:200
  (91 shorter events, 54.1 us)
Async XLA Ops:
  7.2 92.5 %all-gather.5.cloned.1.call-start = ((), (), s32[]{:S(2)}) async-start(), calls=%async_computation.7 | async-start | bytes 2662400 | tf_op jit(solution)/shard_map/all_gather | solution.py:147
  18.2 164.3 %all-gather.3.cloned.1.call-start = ((), (), s32[]{:S(2)}) async-start(), calls=%async_computation.6 | async-start | bytes 2662400 | tf_op jit(solution)/shard_map/all_gather | solution.py:148
  26.7 537.1 %reduce-scatter.5.cloned.1.call-start = ((), (), s32[]{:S(2)}) async-start(), calls=%async_computation.9 | async-start | bytes 5324800 | tf_op jit(solution)/shard_map/reduce_scatter | solution.py:188
  35.7 165.4 %copy-start.3 = (bf16[26,8,8,128]{3,2,1,0:T(8,128)(2,1)}, bf16[26,8,8,128]{3,2,1,0:T(8,128)(2,1)S(1)}, u32[]{:S(2)}) copy-start(bf16[26,8,8,128]{3,2,1,0:T(8,128)(2,1)S(1)} %get-tuple-element.40) | copy-start | bytes 1277956
  35.7 170.8 %copy-start.2 = (bf16[26,8,8,128]{3,2,1,0:T(8,128)(2,1)}, bf16[26,8,8,128]{3,2,1,0:T(8,128)(2,1)S(1)}, u32[]{:S(2)}) copy-start(bf16[26,8,8,128]{3,2,1,0:T(8,128)(2,1)S(1)} %get-tuple-element.39) | copy-start | bytes 1277956
  35.8 157.4 %copy-start.6 = (bf16[26,8,8,128]{3,2,1,0:T(8,128)(2,1)}, bf16[26,8,8,128]{3,2,1,0:T(8,128)(2,1)S(1)}, u32[]{:S(2)}) copy-start(bf16[26,8,8,128]{3,2,1,0:T(8,128)(2,1)S(1)} %get-tuple-element.41) | copy-start | bytes 1277956
  35.8 157.4 %copy-start.5 = (bf16[26,8,8,128]{3,2,1,0:T(8,128)(2,1)}, bf16[26,8,8,128]{3,2,1,0:T(8,128)(2,1)S(1)}, u32[]{:S(2)}) copy-start(bf16[26,8,8,128]{3,2,1,0:T(8,128)(2,1)S(1)} %get-tuple-element.42) | copy-start | bytes 1277956
  185.2 15.9 %copy-start.4 = (bf16[1664,256]{1,0:T(8,128)(2,1)}, bf16[1664,256]{1,0:T(8,128)(2,1)S(1)}, u32[]{:S(2)}) copy-start(bf16[1664,256]{1,0:T(8,128)(2,1)S(1)} %pad_maximum_fusion.3) | copy-start | bytes 2555908
  201.1 7.3 copy-start.9
  213.5 5.5 copy-start.7
  217.9 733.7 %reduce-scatter.3.cloned.1.call-start = ((), (), s32[]{:S(2)}) async-start(), calls=%async_computation.8 | async-start | bytes 5324800 | tf_op jit(solution)/shard_map/reduce_scatter | solution.py:182
  220.1 30.0 %copy-start = (bf16[1664,256]{1,0:T(8,128)(2,1)}, bf16[1664,256]{1,0:T(8,128)(2,1)S(1)}, u32[]{:S(2)}) copy-start(bf16[1664,256]{1,0:T(8,128)(2,1)S(1)} %pad_maximum_fusion.2) | copy-start | bytes 2555908
  292.0 6.5 copy-start.1
  325.6 20.6 %copy-start.8 = (f32[208]{0:T(256)S(1)}, f32[208]{0:T(256)}, u32[]{:S(2)}) copy-start(f32[208]{0:T(256)} %get-tuple-element.36) | copy-start | bytes 2500
  565.3 387.8 %all-to-all-start.3 = ((bf16[4,4,256]{2,1,0:T(4,128)(2,1)}), bf16[4,4,256]{2,1,0:T(4,128)(2,1)S(1)}, u32[]{:S(2)}, u32[]{:S(2)}) async-start(bf16[4,4,256]{2,1,0:T(4,128)(2,1)} %all_to_all.68), calls=%async_computation.5 | async-start | bytes 16384 | tf_op jit(solution)/shard_map/all_to_all | solution.py:203
  953.1 67.2 %all-to-all-start.2 = ((bf16[4,4,256]{2,1,0:T(4,128)(2,1)}), bf16[4,4,256]{2,1,0:T(4,128)(2,1)S(1)}, u32[]{:S(2)}, u32[]{:S(2)}) async-start(bf16[4,4,256]{2,1,0:T(4,128)(2,1)} %all_to_all.64), calls=%async_computation.3 | async-start | bytes 16384 | tf_op jit(solution)/shard_map/all_to_all | solution.py:200
Sparse Core Ops, SparseCore 0:
  18.3 81.2 all-gather.4
  103.5 78.9 all-gather.2
  218.1 345.6 reduce-scatter.4
  566.2 385.3 reduce-scatter.2
where the time goes:
time: 1030 us
  waiting for transfers between devices  693 us (67%)
  matrix products  131 us (13%)
  starting transfers between devices  107 us (10%)
  local copies, waits for them, and re-layouts  40.1 us (4%)
  other arithmetic  27 us (3%)
  blocking collectives  16.6 us (2%)
  between operations  14.7 us (1%)
    reduce_scatter x1, waiting for transfers between devices, local(): lax.psum_scatter(owner_rows(root_key_terms, branch_key_terms, leaf_count,...  334 us
    reduce_scatter x1, waiting for transfers between devices, local(): lax.psum_scatter(owner_rows(root_value_terms, branch_value_terms, leaf_co...  215 us
    all_gather x1, waiting for transfers between devices, local(): lax.all_gather(jnp.concatenate([root_values, branch_value], 0), 'leaf', a...  81.8 us
    all_gather x1, waiting for transfers between devices, local(): lax.all_gather(jnp.concatenate([root_keys, branch_key], 0), 'leaf', axis=...  61.1 us
    all_to_all x1, starting transfers between devices, local(): lax.all_to_all(root_key_sum.astype(jnp.bfloat16), 'head', split_axis=0, c...  54.4 us
    all_to_all x1, starting transfers between devices, local(): lax.all_to_all(root_value_sum.astype(jnp.bfloat16), 'head', split_axis=0,...  51.9 us
    dot_general x2, matrix products, group_terms(): jnp.einsum('gqn,qgd->nd', score_grad, query, preferred_element_type=jnp.f...  45.9 us
    dot_general x2, matrix products, group_terms(): jnp.einsum('gqn,nd->qgd', score_grad, key, preferred_element_type=jnp.flo...  37.7 us
  transfers between devices with their start and end apart: 6, of which 4 were waited for; matrix products, arithmetic and copies ran while one was open for 15% of the time, Pallas kernels for 0%

commit v1 on v0

v1 whole, which is shorter than its diff:
```python
import functools, math
import jax, jax.numpy as jnp
from jax import lax
from jax.experimental import pallas as pl
from jax.experimental.pallas import tpu as pltpu
from jax.sharding import Mesh, PartitionSpec as P

D = 128
HG = 8
GROUP = 8
ROOT, BRANCH, LEAF = 1024, 512, 128
KEYS = ROOT + BRANCH + LEAF
NEG = -1e30
bf16, f32, i32 = jnp.bfloat16, jnp.float32, jnp.int32
SCALE = 1.0 / math.sqrt(D)
C2 = SCALE * math.log2(math.e)
NT = (((1,), (1,)), ((), ()))
NN = (((1,), (0,)), ((), ()))
CH = 256


def dot(a, b, dims=NN):
    return lax.dot_general(a, b, dims, preferred_element_type=f32)


def chunks(n):
    return [(a, min(CH, n - a)) for a in range(0, n, CH)]


def attend_kernel(place, rq, bq, lq, rg, bg, lg, r0, r1, r2, r3, b0, b1, lk, lv, *rest):
    (ra, ba, la, rdq, bdq, ldq, ldk, ldv, r0o, r1o, r2o, r3o, b0o, b1o,
     kk, vv, kt, vt, ss, dd, ak, av) = rest[-22:]
    y, x, z = place[0], place[1], place[2]
    branch_live, leaf_live = place[3], place[4]
    within = (x & 1) * 4 + z
    leaf_index = y * 16 + x * 4 + z
    for i, r in enumerate((r0, r1, r2, r3)):
        kk[i * 256:(i + 1) * 256, :] = r[:, :D]
        vv[i * 256:(i + 1) * 256, :] = r[:, D:]
    for i, r in enumerate((b0, b1)):
        kk[ROOT + i * 256:ROOT + (i + 1) * 256, :] = r[:, :D]
        vv[ROOT + i * 256:ROOT + (i + 1) * 256, :] = r[:, D:]
    kk[ROOT + BRANCH:, :] = lk[...]
    vv[ROOT + BRANCH:, :] = lv[...]
    for a, n in chunks(KEYS):
        kt[:, a:a + n] = kk[a:a + n, :].astype(f32).T.astype(bf16)
        vt[:, a:a + n] = vv[a:a + n, :].astype(f32).T.astype(bf16)
    ak[...] = jnp.zeros_like(ak)
    av[...] = jnp.zeros_like(av)

    def root_pos(a, n, N):
        r = lax.broadcasted_iota(i32, (n, N), 0) + a
        return (((y - (r >> 8)) & 3) << 8) | (((x - (r >> 6)) & 3) << 6) | (r & 63)

    def branch_pos(a, n, N):
        r = lax.broadcasted_iota(i32, (n, N), 0) + a
        return (((x ^ (r >> 8)) & 1) << 8) | (((z - (r >> 6)) & 3) << 6) | (r & 63)

    def tile(q, do, nk, tok, live_col, mask):
        N = q.shape[0]
        m = jnp.full((1, N), NEG, f32)
        for a, n in chunks(nk):
            s = dot(kk[a:a + n, :], q, NT) * C2
            ok = mask(a, n, N)
            if ok is not None:
                s = jnp.where(ok, s, NEG)
            ss[a:a + n, :N] = s
            m = jnp.maximum(m, jnp.max(s, axis=0, keepdims=True))
            dd[a:a + n, :N] = dot(vv[a:a + n, :], do, NT)
        l = jnp.zeros((1, N), f32)
        dl = jnp.zeros((1, N), f32)
        for a, n in chunks(nk):
            e = jnp.exp2(ss[a:a + n, :N] - m)
            ss[a:a + n, :N] = e
            l = l + jnp.sum(e, axis=0, keepdims=True)
            dl = dl + jnp.sum(e * dd[a:a + n, :N], axis=0, keepdims=True)
        inv = 1.0 / l
        delta = dl * inv
        ot = jnp.zeros((D, N), f32)
        qt = jnp.zeros((D, N), f32)
        for a, n in chunks(nk):
            w = ss[a:a + n, :N] * inv
            p = w.astype(bf16)
            ds = (w * (dd[a:a + n, :N] - delta)).astype(bf16)
            av[a:a + n, :] += dot(p, do)
            ak[a:a + n, :] += dot(ds, q)
            ot = ot + dot(vt[:, a:a + n], p)
            qt = qt + dot(kt[:, a:a + n], ds)
        o = jnp.where(live_col, ot, 0.0).T.astype(bf16)
        dq = (qt * SCALE).T.astype(bf16)
        return o, dq

    def grab(ref, heads):
        return jnp.concatenate([ref[:, h] for h in heads], axis=0)

    def leaf_mask(a, n, N):
        if a < ROOT:
            return None
        if a < ROOT + BRANCH:
            return branch_pos(a - ROOT, n, N) < branch_live
        k = lax.broadcasted_iota(i32, (n, N), 0)
        t = lax.broadcasted_iota(i32, (n, N), 1) & (LEAF - 1)
        return (k < leaf_live) & (k <= t)

    def leaf_body(i, c):
        hs = [pl.ds(pl.multiple_of((2 * i + j) * D, D), D) for j in range(2)]
        tok = lax.broadcasted_iota(i32, (2 * LEAF, 1), 0) & (LEAF - 1)
        q = grab(lq, hs)
        do = jnp.where(tok < leaf_live, grab(lg, hs), jnp.zeros((), bf16))
        col = lax.broadcasted_iota(i32, (1, 2 * LEAF), 1) & (LEAF - 1)
        o, dq = tile(q, do, KEYS, tok, col < leaf_live, leaf_mask)
        for j, h in enumerate(hs):
            la[:, h] = o[j * LEAF:(j + 1) * LEAF]
            ldq[:, h] = dq[j * LEAF:(j + 1) * LEAF]
        return c
    lax.fori_loop(0, HG // 2, leaf_body, 0)

    BT = 64
    def branch_mask(a, n, N):
        if a < ROOT:
            return None
        p = branch_pos(a - ROOT, n, N)
        t = (lax.broadcasted_iota(i32, (n, N), 1) & (BT - 1)) + within * BT
        return (p < branch_live) & (p <= t)

    def branch_body(i, c):
        hs = [pl.ds(pl.multiple_of((4 * i + j) * D, D), D) for j in range(4)]
        tok = (lax.broadcasted_iota(i32, (4 * BT, 1), 0) & (BT - 1)) + within * BT
        q = grab(bq, hs)
        do = jnp.where(tok < branch_live, grab(bg, hs), jnp.zeros((), bf16))
        col = (lax.broadcasted_iota(i32, (1, 4 * BT), 1) & (BT - 1)) + within * BT
        o, dq = tile(q, do, ROOT + BRANCH, tok, col < branch_live, branch_mask)
        for j, h in enumerate(hs):
            ba[:, h] = o[j * BT:(j + 1) * BT]
            bdq[:, h] = dq[j * BT:(j + 1) * BT]
        return c
    lax.fori_loop(0, HG // 4, branch_body, 0)

    RT = 16
    def root_mask(a, n, N):
        t = (lax.broadcasted_iota(i32, (n, N), 1) & (RT - 1)) + leaf_index * RT
        return root_pos(a, n, N) <= t
    hs = [pl.ds(j * D, D) for j in range(HG)]
    q = grab(rq, hs)
    do = grab(rg, hs)
    o, dq = tile(q, do, ROOT, None, lax.broadcasted_iota(i32, (1, HG * RT), 1) >= 0, root_mask)
    for j, h in enumerate(hs):
        ra[:, h] = o[j * RT:(j + 1) * RT]
        rdq[:, h] = dq[j * RT:(j + 1) * RT]

    for i, r in enumerate((r0o, r1o, r2o, r3o)):
        s = slice(i * 256, (i + 1) * 256)
        r[:, :D] = (ak[s, :] * SCALE).astype(r.dtype)
        r[:, D:] = av[s, :].astype(r.dtype)
    for i, r in enumerate((b0o, b1o)):
        s = slice(ROOT + i * 256, ROOT + (i + 1) * 256)
        r[:, :D] = (ak[s, :] * SCALE).astype(r.dtype)
        r[:, D:] = av[s, :].astype(r.dtype)
    ldk[...] = (ak[ROOT + BRANCH:, :] * SCALE).astype(bf16)
    ldv[...] = av[ROOT + BRANCH:, :].astype(bf16)


def attend(g, place, queries, grads, roots, branch, lk, lv, prev=None):
    W = HG * D
    def col(rows, w):
        return pl.BlockSpec((rows, w), lambda i: (0, g))
    def whole(shape):
        return pl.BlockSpec(shape, lambda i: (0, 0))
    in_specs = [pl.BlockSpec(memory_space=pltpu.SMEM)]
    in_specs += [col(n, W) for n in (16, 64, 128)] * 2
    in_specs += [whole((256, 2 * D))] * 4 + [col(256, 2 * D)] * 2
    in_specs += [col(LEAF, D)] * 2
    args = [place, *queries, *grads, *roots, *branch, lk, lv]
    alias = {}
    if prev is not None:
        for i, p in enumerate(prev):
            alias[len(args)] = i
            args.append(p)
            in_specs.append(pl.BlockSpec(memory_space=pl.ANY))
    S = jax.ShapeDtypeStruct
    outs = [S((n, 2 * W), bf16) for n in (16, 64, 128)] * 2 + [S((LEAF, 2 * D), bf16)] * 2
    out_specs = [col(n, W) for n in (16, 64, 128)] * 2 + [col(LEAF, D)] * 2
    outs += [S((256, 2 * D), f32)] + [S((256, 2 * D), bf16)] * 3
    out_specs += [whole((256, 2 * D))] * 4
    outs += [S((256, 2 * D), f32), S((256, 2 * D), bf16)]
    out_specs += [whole((256, 2 * D))] * 2
    scratch = [pltpu.VMEM((KEYS, D), bf16)] * 2 + [pltpu.VMEM((D, KEYS), bf16)] * 2
    scratch += [pltpu.VMEM((KEYS, 256), f32)] * 2 + [pltpu.VMEM((KEYS, D), f32)] * 2
    return pl.pallas_call(
        attend_kernel, grid=(1,), out_shape=outs, in_specs=in_specs, out_specs=out_specs,
        scratch_shapes=scratch, input_output_aliases=alias,
        compiler_params=pltpu.CompilerParams(vmem_limit_bytes=40 * 2**20),
        cost_estimate=pl.CostEstimate(flops=2 * 6 * 1664 * 1664 * 128, bytes_accessed=6 * 2**20, transcendentals=1664 * 1664),
        name="attend",
    )(*args)


def split_rows(r0, r1, r2, r3, o0, o1):
    n = r0.shape[0]
    for i, r in enumerate((r0, r1, r2, r3)):
        o0[i * n:(i + 1) * n, :] = r[:, :2 * D]
        o1[i * n:(i + 1) * n, :] = r[:, 2 * D:]


def stack_rows(r0, r1, r2, r3, o):
    n = r0.shape[0]
    for i, r in enumerate((r0, r1, r2, r3)):
        o[i * n:(i + 1) * n, :] = r[...]


def add_y(own0, a1, a2, a3, own1, c1, c2, c3, o0, o1, o2, o3):
    n = own0.shape[0] // 4
    for j, (own, *parts) in enumerate(((own0, a1, a2, a3), (own1, c1, c2, c3))):
        for i, o in enumerate((o0, o1, o2, o3)):
            s = slice(i * n, (i + 1) * n)
            t = own[s, :]
            for p in parts:
                t = t + p[s, :].astype(f32)
            o[:, j * 2 * D:(j + 1) * 2 * D] = t.astype(o.dtype)


def add_pair(own0, a1, own1, c1, o0, o1, o2, o3):
    n = own0.shape[0] // 4
    for j, (own, p) in enumerate(((own0, a1), (own1, c1))):
        for i, o in enumerate((o0, o1, o2, o3)):
            s = slice(i * n, (i + 1) * n)
            o[:, j * 2 * D:(j + 1) * 2 * D] = (own[s, :] + p[s, :].astype(f32)).astype(o.dtype)


def add_x(own, a1, a2, a3, o):
    o[...] = own[...] + a1[...].astype(f32) + a2[...].astype(f32) + a3[...].astype(f32)


def add_z(own, a1, a2, a3, ok, ov):
    t = own[...] + a1[...].astype(f32) + a2[...].astype(f32) + a3[...].astype(f32)
    for g in range(2):
        ok[:, g * D:(g + 1) * D] = t[:, 2 * g * D:(2 * g + 1) * D].astype(ok.dtype)
        ov[:, g * D:(g + 1) * D] = t[:, (2 * g + 1) * D:(2 * g + 2) * D].astype(ov.dtype)


def small(body, outs, *args):
    return pl.pallas_call(
        body,
        out_shape=[jax.ShapeDtypeStruct(s, t) for s, t in outs],
        in_specs=[pl.BlockSpec(memory_space=pltpu.VMEM)] * len(args),
        out_specs=[pl.BlockSpec(memory_space=pltpu.VMEM)] * len(outs),
        cost_estimate=pl.CostEstimate(flops=10**6, bytes_accessed=2**20, transcendentals=0),
    )(*args)


def shift(a, axis, d):
    return lax.ppermute(a, axis, [(i, (i + d) % 4) for i in range(4)])


def shifts(a, axis):
    return [shift(a, axis, d) for d in (1, 2, 3)]


def back(parts, axis):
    return [shift(p, axis, -d) for d, p in zip((1, 2, 3), parts)]


def pair(a):
    return lax.ppermute(a, "x", [(i, i ^ 1) for i in range(4)])


def local(
    root_query, branch_query, leaf_query, root_key, root_value, branch_key, branch_value,
    leaf_key, leaf_value, root_grad_out, branch_grad_out, leaf_grad_out,
    branch_lengths, leaf_lengths,
):
    y, x, z = (lax.axis_index(a) for a in ("y", "x", "z"))
    branch_live = branch_lengths[(y * 16 + x * 4 + z) // GROUP]
    place = jnp.stack([y, x, z, branch_live, leaf_lengths[0]]).astype(i32)
    queries = (root_query, branch_query, leaf_query)
    grads = (root_grad_out, branch_grad_out, leaf_grad_out)

    raw = jnp.stack([root_key.reshape(4, 4, 2, D), root_value.reshape(4, 4, 2, D)], 3)
    raw = raw.reshape(4, 4, 4 * D).transpose(1, 0, 2)
    raw = jnp.broadcast_to(raw[None], (4, 4, 4, 4 * D)).reshape(16, 4, 4 * D)
    own = lax.all_to_all(raw, ("z", "head"), 0, 0, tiled=True).reshape(64, 4 * D)
    r0, r1 = small(split_rows, [((256, 2 * D), bf16)] * 2, own, *shifts(own, "x"))

    mine = jnp.stack([branch_key.reshape(64, 2, D), branch_value.reshape(64, 2, D)], 2)
    mine = mine.reshape(64, 4 * D)
    b_own, = small(stack_rows, [((256, 4 * D), bf16)], mine, *shifts(mine, "z"))
    branch = (b_own, pair(b_own))

    roots0 = [r0, *shifts(r0, "y")]
    r1, *roots0 = lax.optimization_barrier((r1, *roots0))
    roots1 = [r1, *shifts(r1, "y")]

    first = attend(0, place, queries, grads, roots0, branch, leaf_key, leaf_value)
    ry0 = back(first[9:12], "y")
    bx0 = pair(first[13])
    second = attend(1, place, queries, grads, roots1, branch, leaf_key, leaf_value, first[:8])
    y1, b1, *rest = lax.optimization_barrier((second[9:12], second[13], *ry0, bx0))
    ry0, bx0 = rest[:3], rest[3]
    ry1 = back(y1, "y")
    bx1 = pair(b1)
    own, *parts = small(
        add_y, [((64, 4 * D), f32)] + [((64, 4 * D), bf16)] * 3,
        first[8], *ry0, second[8], *ry1,
    )
    sums, = small(add_x, [((64, 4 * D), f32)], own, *back(parts, "x"))
    own, *parts = small(
        add_pair, [((64, 4 * D), f32)] + [((64, 4 * D), bf16)] * 3,
        first[12], bx0, second[12], bx1,
    )
    bk, bv = small(add_z, [((64, 2 * D), bf16)] * 2, own, *back(parts, "z"))
    last = lax.all_to_all(sums.reshape(16, 4, 4 * D), ("z", "head"), 0, 0, tiled=True)
    last = jnp.sum(last.reshape(4, 4, 4, 2, 2, D), 0).astype(bf16)
    rk = last[:, :, :, 0].transpose(1, 0, 2, 3).reshape(4, 8 * D)
    rv = last[:, :, :, 1].transpose(1, 0, 2, 3).reshape(4, 8 * D)
    ra, ba, la, rdq, bdq, ldq, ldk, ldv = second[:8]
    return ra, ba, la, rdq, bdq, ldq, rk, rv, bk, bv, ldk, ldv


def solution(mesh):
    fine = Mesh(mesh.devices.reshape(4, 4, 4, 4), ("y", "x", "z", "head"))
    leaf = ("y", "x", "z")
    both, rows = P(leaf, "head"), P((*leaf, "head"), None)
    return jax.shard_map(
        local,
        mesh=fine,
        in_specs=(both, both, both, rows, rows, both, both, both, both, both, both, both, P(), P(leaf)),
        out_specs=(both, both, both, both, both, both, rows, rows, both, both, both, both),
        check_vma=False,
    )
```

time: 1030 us -> 152 us (0.15)
  waiting for transfers between devices: 693 us -> 35.4 us
  matrix products: 131 us -> 0 us
  starting transfers between devices: 107 us -> 54.4 us
  Pallas kernels: 0 us -> 39.6 us
  other arithmetic: 27 us -> 0.23 us
  local copies, waits for them, and re-layouts: 40.1 us -> 18.9 us
  blocking collectives: 16.6 us -> 0 us
  between operations: 14.7 us -> 1.67 us
    reduce_scatter x2 -> x0, waiting for transfers between devices: 550 us -> none  [the longest x1 334 us: local(): lax.psum_scatter(owner_rows(root_key_terms, branch_key_terms, leaf_count,...]
    all_gather x2 -> x0, waiting for transfers between devices: 143 us -> none  [the longest x1 81.8 us: local(): lax.all_gather(jnp.concatenate([root_values, branch_value], 0), 'leaf', a...]
    dot_general x10 -> x0, matrix products: 115 us -> none  [the longest x2 45.9 us: group_terms(): jnp.einsum('gqn,qgd->nd', score_grad, query, preferred_element_type=jnp.f...]
    all_to_all x2, starting transfers between devices: 106 us -> 16.3 us  [the longest x1 10.3 us: local(): lax.all_to_all(sums.reshape(16, 4, 4 * D), ('z', 'head'), 0, 0, tiled=True)]
    pallas_call x0 -> x8, Pallas kernels: none -> 39.6 us  [the longest x2 29 us: attend(): pl.pallas_call(attend_kernel, grid=(1,), out_shape=outs, in_specs=in_spec...]
    ppermute x0 -> x27, starting transfers between devices: none -> 38.1 us  [the longest x24 36.8 us: shift(): return lax.ppermute(a, axis, [(i, (i + d) % 4) for i in range(4)])]
    ppermute x0 -> x27, waiting for transfers between devices: none -> 31.8 us  [the longest x24 26.9 us: shift(): return lax.ppermute(a, axis, [(i, (i + d) % 4) for i in range(4)])]
    slice x17 -> x1, local copies, waits for them, and re-layouts: 22.4 us -> 0.03 us  [local(): rv = last[:, :, :, 1].transpose(1, 0, 2, 3).reshape(4, 8 * D)]
  transfers between devices with their start and end apart: 6 -> 29, of which waited for: 4 -> 16; matrix products, arithmetic and copies ran while one was open for 15% -> 2% of each run, Pallas kernels for 0% -> 24%
where the time goes in v1:
time: 152 us; the launch traced here: 150 us
  starting transfers between devices  54.4 us (36%)
  Pallas kernels  39.6 us (26%)
  waiting for transfers between devices  35.4 us (23%)
  local copies, waits for them, and re-layouts  18.9 us (12%)
  between operations  1.67 us (1%)
    ppermute x24, starting transfers between devices, shift(): return lax.ppermute(a, axis, [(i, (i + d) % 4) for i in range(4)])  36.8 us
    pallas_call x2, Pallas kernels, attend(): pl.pallas_call(attend_kernel, grid=(1,), out_shape=outs, in_specs=in_spec...  29 us
    ppermute x24, waiting for transfers between devices, shift(): return lax.ppermute(a, axis, [(i, (i + d) % 4) for i in range(4)])  26.9 us
    unnamed x80, local copies, waits for them, and re-layouts  11.6 us
    pallas_call x6, Pallas kernels, small(): pl.pallas_call(body, out_shape=[jax.ShapeDtypeStruct(s, t) for s, t in ou...  10.6 us
    all_to_all x1, starting transfers between devices, local(): lax.all_to_all(sums.reshape(16, 4, 4 * D), ('z', 'head'), 0, 0, tiled=True)  10.3 us
    all_to_all x1, starting transfers between devices, local(): lax.all_to_all(raw, ('z', 'head'), 0, 0, tiled=True).reshape(64, 4 * D)  5.94 us
    ppermute x3, waiting for transfers between devices, pair(): return lax.ppermute(a, 'x', [(i, i ^ 1) for i in range(4)])  4.92 us
  transfers between devices with their start and end apart: 29, of which 16 were waited for; matrix products, arithmetic and copies ran while one was open for 2% of the time, Pallas kernels for 24%

profile of v1, /device:TPU:1, one launch (start us, length us, event | category | flops | bytes accessed | tf_op | source)
XLA Modules:
  0.0 150.2 jit_solution(14811509616547842475)
XLA Ops:
  1.7 6.9 %collective-permute-start.11 = (bf16[64,512]{1,0:T(8,128)(2,1)S(1)}, bf16[64,512]{1,0:T(8,128)(2,1)S(1)}, u32[]{:S(2)}, u32[]{:S(2)}) collective-permute-start(bf16[64,512]{1,0:T(8,128)(2,1)S(1)} %reshape.52.r0), channel_id=1, source_target_pairs={{0,12},{4,0},{8,4},{12,8},{1,13},{5,1},{9,5},{13,9},{2,14},{6,2},{... | collective-permute-start | bytes 196616 | tf_op jit(solution)/shard_map/ppermute | solution.py:252
  9.7 2.3 %collective-permute-start.9 = (bf16[64,512]{1,0:T(8,128)(2,1)S(1)}, bf16[64,512]{1,0:T(8,128)(2,1)S(1)}, u32[]{:S(2)}, u32[]{:S(2)}) collective-permute-start(bf16[64,512]{1,0:T(8,128)(2,1)S(1)} %reshape.52.r0), channel_id=1, source_target_pairs={{0,4},{4,8},{8,12},{12,0},{1,5},{5,9},{9,13},{13,1},{2,6},{6,10},{... | collective-permute-start | bytes 196616 | tf_op jit(solution)/shard_map/ppermute | solution.py:252
  14.1 5.9 %all-to-all-start = ((bf16[16,4,512]{2,1,0:T(4,128)(2,1)}), bf16[16,4,512]{2,1,0:T(4,128)(2,1)S(1)}, u32[]{:S(2)}, u32[]{:S(2)}) async-start(bf16[16,4,512]{2,1,0:T(4,128)(2,1)} %bitcast.5), calls=%async_computation | async-start | bytes 131072 | tf_op jit(solution)/shard_map/all_to_all | solution.py:281
  24.3 3.6 %all-to-all-done = bf16[16,4,512]{2,1,0:T(4,128)(2,1)S(1)} async-done(((bf16[16,4,512]{2,1,0:T(4,128)(2,1)}), bf16[16,4,512]{2,1,0:T(4,128)(2,1)S(1)}, u32[]{:S(2)}, u32[]{:S(2)}) %all-to-all-start) | async-done | bytes 65568 | tf_op jit(solution)/shard_map/all_to_all | solution.py:281
  27.9 2.6 %collective-permute-start.2 = (bf16[64,512]{1,0:T(8,128)(2,1)S(1)}, bf16[64,512]{1,0:T(8,128)(2,1)S(1)}, u32[]{:S(2)}, u32[]{:S(2)}) collective-permute-start(bf16[64,512]{1,0:T(8,128)(2,1)S(1)} %reshape.51.r0), channel_id=1, source_target_pairs={{0,48},{16,0},{32,16},{48,32},{1,49},{17,1},{33,17},{49,33},{2,50}... | collective-permute-start | bytes 196616 | tf_op jit(solution)/shard_map/ppermute | solution.py:252
  32.5 2.6 %collective-permute-done.1.r2 = bf16[64,512]{1,0:T(8,128)(2,1)S(1)} collective-permute-done((bf16[64,512]{1,0:T(8,128)(2,1)S(1)}, bf16[64,512]{1,0:T(8,128)(2,1)S(1)}, u32[]{:S(2)}, u32[]{:S(2)}) %collective-permute-start.1) | collective-permute-done | bytes 65568 | tf_op jit(solution)/shard_map/ppermute | solution.py:252
  39.3 2.7 %collective-permute-start.5 = (bf16[256,256]{1,0:T(8,128)(2,1)}, bf16[256,256]{1,0:T(8,128)(2,1)S(1)}, u32[]{:S(2)}, u32[]{:S(2)}) collective-permute-start(bf16[256,256]{1,0:T(8,128)(2,1)} %get-tuple-element.68.r0), channel_id=1, source_target_pairs={{0,192},{64,0},{128,64},{192,128},{1,193},{65,1},{129,65},{193,129... | collective-permute-start | bytes 393224 | tf_op jit(solution)/shard_map/ppermute | solution.py:252
  45.0 2.2 %collective-permute-done.5.r3 = bf16[256,256]{1,0:T(8,128)(2,1)S(1)} collective-permute-done((bf16[256,256]{1,0:T(8,128)(2,1)}, bf16[256,256]{1,0:T(8,128)(2,1)S(1)}, u32[]{:S(2)}, u32[]{:S(2)}) %collective-permute-start.5) | collective-permute-done | bytes 131104 | tf_op jit(solution)/shard_map/ppermute | solution.py:252
  47.7 3.9 %collective-permute-done.3.r1 = bf16[256,256]{1,0:T(8,128)(2,1)S(1)} collective-permute-done((bf16[256,256]{1,0:T(8,128)(2,1)}, bf16[256,256]{1,0:T(8,128)(2,1)S(1)}, u32[]{:S(2)}, u32[]{:S(2)}) %collective-permute-start.3) | collective-permute-done | bytes 131104 | tf_op jit(solution)/shard_map/ppermute | solution.py:252
  57.4 14.5 %attend.2 = (bf16[16,2048]{1,0:T(8,128)(2,1)}, bf16[64,2048]{1,0:T(8,128)(2,1)}, bf16[128,2048]{1,0:T(8,128)(2,1)}, bf16[16,2048]{1,0:T(8,128)(2,1)}, bf16[64,20...) custom-call(s32[5]{0:T(128)S(1)} %stack.21.place, ...), custom_call_target="tpu_custom_call" | custom-call | flops 4253024256 | bytes 6291456 | tf_op jit(solution)/shard_map/attend/pallas_call | solution.py:189
  73.3 2.4 %collective-permute-start.13 = (bf16[256,256]{1,0:T(8,128)(2,1)S(1)}, bf16[256,256]{1,0:T(8,128)(2,1)S(1)}, u32[]{:S(2)}, u32[]{:S(2)}) collective-permute-start(bf16[256,256]{1,0:T(8,128)(2,1)S(1)} %get-tuple-element.91), channel_id=1, source_target_pairs={{0,192},{64,0},{128,64},{192,128},{1,193},{65,1},{129,65},{193,129... | collective-permute-start | bytes 393224 | tf_op jit(solution)/shard_map/ppermute | solution.py:252
  77.8 14.5 %attend.3 = (bf16[16,2048]{1,0:T(8,128)(2,1)}, bf16[64,2048]{1,0:T(8,128)(2,1)}, bf16[128,2048]{1,0:T(8,128)(2,1)}, bf16[16,2048]{1,0:T(8,128)(2,1)}, bf16[64,20...) custom-call(s32[5]{0:T(128)S(1)} %stack.21.place, ...), custom_call_target="tpu_custom_call", output_to_operand_aliasing={{0}: (15, {}), {1}: (16, {}), {2}: (17, {}), {3}: (18, {}),... | custom-call | flops 4253024256 | bytes 6291456 | tf_op jit(solution)/shard_map/attend/pallas_call | solution.py:189
  96.4 2.6 %collective-permute-done.17.c1 = bf16[256,256]{1,0:T(8,128)(2,1)S(1)} collective-permute-done((bf16[256,256]{1,0:T(8,128)(2,1)S(1)}, bf16[256,256]{1,0:T(8,128)(2,1)S(1)}, u32[]{:S(2)}, u32[]{:S(2)}) %collective-permute-start.17) | collective-permute-done | bytes 131104 | tf_op jit(solution)/shard_map/ppermute | solution.py:252
  99.0 2.1 %collective-permute-done.18.c2 = bf16[256,256]{1,0:T(8,128)(2,1)S(1)} collective-permute-done((bf16[256,256]{1,0:T(8,128)(2,1)S(1)}, bf16[256,256]{1,0:T(8,128)(2,1)S(1)}, u32[]{:S(2)}, u32[]{:S(2)}) %collective-permute-start.18) | collective-permute-done | bytes 131104 | tf_op jit(solution)/shard_map/ppermute | solution.py:252
  103.1 2.1 %shard_map.231 = (f32[64,512]{1,0:T(8,128)}, bf16[64,512]{1,0:T(8,128)(2,1)}, bf16[64,512]{1,0:T(8,128)(2,1)}, bf16[64,512]{1,0:T(8,128)(2,1)}) custom-call(f32[256,256]{1,0:T(8,128)} %copy-done.2, bf16[256,256]{1,0:T(8,128)(2,1)} %copy-done.18, bf16[256,256]{1,0:T(8,128)(2,1)} %copy-done.19, bf16[256,256]{1,0:T(8,128)(2,1)} %copy-done.20, ...), custom_call_target="tpu_custom_call" | custom-call | flops 1000000 | bytes 1048576 | tf_op jit(solution)/shard_map/pallas_call | solution.py:242
  106.0 2.5 %collective-permute-start.21 = (bf16[64,512]{1,0:T(8,128)(2,1)}, bf16[64,512]{1,0:T(8,128)(2,1)S(1)}, u32[]{:S(2)}, u32[]{:S(2)}) collective-permute-start(bf16[64,512]{1,0:T(8,128)(2,1)} %get-tuple-element.104), channel_id=1, source_target_pairs={{0,32},{16,48},{32,0},{48,16},{1,33},{17,49},{33,1},{49,17},{2,34}... | collective-permute-start | bytes 196616 | tf_op jit(solution)/shard_map/ppermute | solution.py:252
  108.6 2.2 %collective-permute-done.21.a2 = bf16[64,512]{1,0:T(8,128)(2,1)S(1)} collective-permute-done((bf16[64,512]{1,0:T(8,128)(2,1)}, bf16[64,512]{1,0:T(8,128)(2,1)S(1)}, u32[]{:S(2)}, u32[]{:S(2)}) %collective-permute-start.21) | collective-permute-done | bytes 65568 | tf_op jit(solution)/shard_map/ppermute | solution.py:252
  110.8 2.2 %collective-permute-done.22.a3 = bf16[64,512]{1,0:T(8,128)(2,1)S(1)} collective-permute-done((bf16[64,512]{1,0:T(8,128)(2,1)}, bf16[64,512]{1,0:T(8,128)(2,1)S(1)}, u32[]{:S(2)}, u32[]{:S(2)}) %collective-permute-start.22) | collective-permute-done | bytes 65568 | tf_op jit(solution)/shard_map/ppermute | solution.py:252
  116.9 10.3 %all-to-all-start.1 = ((f32[16,4,512]{2,1,0:T(4,128)}), f32[16,4,512]{2,1,0:T(4,128)S(1)}, u32[]{:S(2)}, u32[]{:S(2)}) async-start(f32[16,4,512]{2,1,0:T(4,128)} %reshape.53), calls=%async_computation.1 | async-start | bytes 262144 | tf_op jit(solution)/shard_map/all_to_all | solution.py:311
  127.3 4.9 %collective-permute-done.23.c1 = bf16[256,256]{1,0:T(8,128)(2,1)S(1)} collective-permute-done((bf16[256,256]{1,0:T(8,128)(2,1)S(1)}, bf16[256,256]{1,0:T(8,128)(2,1)S(1)}, u32[]{:S(2)}, u32[]{:S(2)}) %collective-permute-start.23) | collective-permute-done | bytes 131104 | tf_op jit(solution)/shard_map/ppermute | solution.py:264
  134.7 3.3 %collective-permute-start.24 = (bf16[64,512]{1,0:T(8,128)(2,1)}, bf16[64,512]{1,0:T(8,128)(2,1)S(1)}, u32[]{:S(2)}, u32[]{:S(2)}) collective-permute-start(bf16[64,512]{1,0:T(8,128)(2,1)} %get-tuple-element.111), channel_id=1, source_target_pairs={{0,12},{4,0},{8,4},{12,8},{1,13},{5,1},{9,5},{13,9},{2,14},{6,2},{... | collective-permute-start | bytes 196616 | tf_op jit(solution)/shard_map/ppermute | solution.py:252
  138.0 2.1 %collective-permute-start.25 = (bf16[64,512]{1,0:T(8,128)(2,1)}, bf16[64,512]{1,0:T(8,128)(2,1)S(1)}, u32[]{:S(2)}, u32[]{:S(2)}) collective-permute-start(bf16[64,512]{1,0:T(8,128)(2,1)} %get-tuple-element.112), channel_id=1, source_target_pairs={{0,8},{4,12},{8,0},{12,4},{1,9},{5,13},{9,1},{13,5},{2,10},{6,14},... | collective-permute-start | bytes 196616 | tf_op jit(solution)/shard_map/ppermute | solution.py:252
  140.1 2.1 %collective-permute-start.26 = (bf16[64,512]{1,0:T(8,128)(2,1)}, bf16[64,512]{1,0:T(8,128)(2,1)S(1)}, u32[]{:S(2)}, u32[]{:S(2)}) collective-permute-start(bf16[64,512]{1,0:T(8,128)(2,1)} %get-tuple-element.113), channel_id=1, source_target_pairs={{0,4},{4,8},{8,12},{12,0},{1,5},{5,9},{9,13},{13,1},{2,6},{6,10},{... | collective-permute-start | bytes 196616 | tf_op jit(solution)/shard_map/ppermute | solution.py:252
  142.2 3.1 %collective-permute-done.25.a2 = bf16[64,512]{1,0:T(8,128)(2,1)S(1)} collective-permute-done((bf16[64,512]{1,0:T(8,128)(2,1)}, bf16[64,512]{1,0:T(8,128)(2,1)S(1)}, u32[]{:S(2)}, u32[]{:S(2)}) %collective-permute-start.25) | collective-permute-done | bytes 65568 | tf_op jit(solution)/shard_map/ppermute | solution.py:252
  (143 shorter events, 44.6 us)
Async XLA Ops:
  1.7 18.3 %collective-permute-start.11 = (bf16[64,512]{1,0:T(8,128)(2,1)S(1)}, bf16[64,512]{1,0:T(8,128)(2,1)S(1)}, u32[]{:S(2)}, u32[]{:S(2)}) collective-permute-start(bf16[64,512]{1,0:T(8,128)(2,1)S(1)} %reshape.52.r0), channel_id=1, source_target_pairs={{0,12},{4,0},{8,4},{12,8},{1,13},{5,1},{9,5},{13,9},{2,14},{6,2},{... | collective-permute-start | bytes 196616 | tf_op jit(solution)/shard_map/ppermute | solution.py:252
  8.7 11.4 %collective-permute-start.10 = (bf16[64,512]{1,0:T(8,128)(2,1)S(1)}, bf16[64,512]{1,0:T(8,128)(2,1)S(1)}, u32[]{:S(2)}, u32[]{:S(2)}) collective-permute-start(bf16[64,512]{1,0:T(8,128)(2,1)S(1)} %reshape.52.r0), channel_id=1, source_target_pairs={{0,8},{4,12},{8,0},{12,4},{1,9},{5,13},{9,1},{13,5},{2,10},{6,14},... | collective-permute-start | bytes 196616 | tf_op jit(solution)/shard_map/ppermute | solution.py:252
  9.7 10.5 %collective-permute-start.9 = (bf16[64,512]{1,0:T(8,128)(2,1)S(1)}, bf16[64,512]{1,0:T(8,128)(2,1)S(1)}, u32[]{:S(2)}, u32[]{:S(2)}) collective-permute-start(bf16[64,512]{1,0:T(8,128)(2,1)S(1)} %reshape.52.r0), channel_id=1, source_target_pairs={{0,4},{4,8},{8,12},{12,0},{1,5},{5,9},{9,13},{13,1},{2,6},{6,10},{... | collective-permute-start | bytes 196616 | tf_op jit(solution)/shard_map/ppermute | solution.py:252
  14.1 13.7 %all-to-all-start = ((bf16[16,4,512]{2,1,0:T(4,128)(2,1)}), bf16[16,4,512]{2,1,0:T(4,128)(2,1)S(1)}, u32[]{:S(2)}, u32[]{:S(2)}) async-start(bf16[16,4,512]{2,1,0:T(4,128)(2,1)} %bitcast.5), calls=%async_computation | async-start | bytes 131072 | tf_op jit(solution)/shard_map/all_to_all | solution.py:281
  23.0 30.0 %collective-permute-start.12 = (bf16[256,512]{1,0:T(8,128)(2,1)}, bf16[256,512]{1,0:T(8,128)(2,1)S(1)}, u32[]{:S(2)}, u32[]{:S(2)}) collective-permute-start(bf16[256,512]{1,0:T(8,128)(2,1)} %shard_map.230.b0), channel_id=1, source_target_pairs={{0,16},{16,0},{32,48},{48,32},{1,17},{17,1},{33,49},{49,33},{2,18}... | collective-permute-start | bytes 786440 | tf_op jit(solution)/shard_map/ppermute | solution.py:264
  31.0 6.0 %collective-permute-start = (bf16[64,512]{1,0:T(8,128)(2,1)S(1)}, bf16[64,512]{1,0:T(8,128)(2,1)S(1)}, u32[]{:S(2)}, u32[]{:S(2)}) collective-permute-start(bf16[64,512]{1,0:T(8,128)(2,1)S(1)} %reshape.51.r0), channel_id=1, source_target_pairs={{0,16},{16,32},{32,48},{48,0},{1,17},{17,33},{33,49},{49,1},{2,18}... | collective-permute-start | bytes 196616 | tf_op jit(solution)/shard_map/ppermute | solution.py:252
  39.3 8.0 %collective-permute-start.5 = (bf16[256,256]{1,0:T(8,128)(2,1)}, bf16[256,256]{1,0:T(8,128)(2,1)S(1)}, u32[]{:S(2)}, u32[]{:S(2)}) collective-permute-start(bf16[256,256]{1,0:T(8,128)(2,1)} %get-tuple-element.68.r0), channel_id=1, source_target_pairs={{0,192},{64,0},{128,64},{192,128},{1,193},{65,1},{129,65},{193,129... | collective-permute-start | bytes 393224 | tf_op jit(solution)/shard_map/ppermute | solution.py:252
  42.0 5.6 %collective-permute-start.4 = (bf16[256,256]{1,0:T(8,128)(2,1)}, bf16[256,256]{1,0:T(8,128)(2,1)S(1)}, u32[]{:S(2)}, u32[]{:S(2)}) collective-permute-start(bf16[256,256]{1,0:T(8,128)(2,1)} %get-tuple-element.68.r0), channel_id=1, source_target_pairs={{0,128},{64,192},{128,0},{192,64},{1,129},{65,193},{129,1},{193,65... | collective-permute-start | bytes 393224 | tf_op jit(solution)/shard_map/ppermute | solution.py:252
  42.4 9.2 %collective-permute-start.3 = (bf16[256,256]{1,0:T(8,128)(2,1)}, bf16[256,256]{1,0:T(8,128)(2,1)S(1)}, u32[]{:S(2)}, u32[]{:S(2)}) collective-permute-start(bf16[256,256]{1,0:T(8,128)(2,1)} %get-tuple-element.68.r0), channel_id=1, source_target_pairs={{0,64},{64,128},{128,192},{192,0},{1,65},{65,129},{129,193},{193,1... | collective-permute-start | bytes 393224 | tf_op jit(solution)/shard_map/ppermute | solution.py:252
  51.6 25.3 %collective-permute-start.8 = (bf16[256,256]{1,0:T(8,128)(2,1)}, bf16[256,256]{1,0:T(8,128)(2,1)S(1)}, u32[]{:S(2)}, u32[]{:S(2)}) collective-permute-start(bf16[256,256]{1,0:T(8,128)(2,1)} %get-tuple-element.67.r0), channel_id=1, source_target_pairs={{0,192},{64,0},{128,64},{192,128},{1,193},{65,1},{129,65},{193,129... | collective-permute-start | bytes 393224 | tf_op jit(solution)/shard_map/ppermute | solution.py:252
  51.6 26.1 %collective-permute-start.7 = (bf16[256,256]{1,0:T(8,128)(2,1)}, bf16[256,256]{1,0:T(8,128)(2,1)S(1)}, u32[]{:S(2)}, u32[]{:S(2)}) collective-permute-start(bf16[256,256]{1,0:T(8,128)(2,1)} %get-tuple-element.67.r0), channel_id=1, source_target_pairs={{0,128},{64,192},{128,0},{192,64},{1,129},{65,193},{129,1},{193,65... | collective-permute-start | bytes 393224 | tf_op jit(solution)/shard_map/ppermute | solution.py:252
  51.6 26.1 %collective-permute-start.6 = (bf16[256,256]{1,0:T(8,128)(2,1)}, bf16[256,256]{1,0:T(8,128)(2,1)S(1)}, u32[]{:S(2)}, u32[]{:S(2)}) collective-permute-start(bf16[256,256]{1,0:T(8,128)(2,1)} %get-tuple-element.67.r0), channel_id=1, source_target_pairs={{0,64},{64,128},{128,192},{192,0},{1,65},{65,129},{129,193},{193,1... | collective-permute-start | bytes 393224 | tf_op jit(solution)/shard_map/ppermute | solution.py:252
  73.3 20.4 %collective-permute-start.13 = (bf16[256,256]{1,0:T(8,128)(2,1)S(1)}, bf16[256,256]{1,0:T(8,128)(2,1)S(1)}, u32[]{:S(2)}, u32[]{:S(2)}) collective-permute-start(bf16[256,256]{1,0:T(8,128)(2,1)S(1)} %get-tuple-element.91), channel_id=1, source_target_pairs={{0,192},{64,0},{128,64},{192,128},{1,193},{65,1},{129,65},{193,129... | collective-permute-start | bytes 393224 | tf_op jit(solution)/shard_map/ppermute | solution.py:252
  75.7 18.0 %collective-permute-start.14 = (bf16[256,256]{1,0:T(8,128)(2,1)S(1)}, bf16[256,256]{1,0:T(8,128)(2,1)S(1)}, u32[]{:S(2)}, u32[]{:S(2)}) collective-permute-start(bf16[256,256]{1,0:T(8,128)(2,1)S(1)} %get-tuple-element.92), channel_id=1, source_target_pairs={{0,128},{64,192},{128,0},{192,64},{1,129},{65,193},{129,1},{193,65... | collective-permute-start | bytes 393224 | tf_op jit(solution)/shard_map/ppermute | solution.py:252
  76.9 16.9 %collective-permute-start.15 = (bf16[256,256]{1,0:T(8,128)(2,1)S(1)}, bf16[256,256]{1,0:T(8,128)(2,1)S(1)}, u32[]{:S(2)}, u32[]{:S(2)}) collective-permute-start(bf16[256,256]{1,0:T(8,128)(2,1)S(1)} %get-tuple-element.93), channel_id=1, source_target_pairs={{0,64},{64,128},{128,192},{192,0},{1,65},{65,129},{129,193},{193,1... | collective-permute-start | bytes 393224 | tf_op jit(solution)/shard_map/ppermute | solution.py:252
  77.7 16.0 %collective-permute-start.16 = (bf16[256,256]{1,0:T(8,128)(2,1)S(1)}, bf16[256,256]{1,0:T(8,128)(2,1)S(1)}, u32[]{:S(2)}, u32[]{:S(2)}) collective-permute-start(bf16[256,256]{1,0:T(8,128)(2,1)S(1)} %get-tuple-element.94), channel_id=1, source_target_pairs={{0,16},{16,0},{32,48},{48,32},{1,17},{17,1},{33,49},{49,33},{2,18}... | collective-permute-start | bytes 393224 | tf_op jit(solution)/shard_map/ppermute | solution.py:264
  93.8 5.2 %collective-permute-start.17 = (bf16[256,256]{1,0:T(8,128)(2,1)S(1)}, bf16[256,256]{1,0:T(8,128)(2,1)S(1)}, u32[]{:S(2)}, u32[]{:S(2)}) collective-permute-start(bf16[256,256]{1,0:T(8,128)(2,1)S(1)} %get-tuple-element.99), channel_id=1, source_target_pairs={{0,192},{64,0},{128,64},{192,128},{1,193},{65,1},{129,65},{193,129... | collective-permute-start | bytes 393224 | tf_op jit(solution)/shard_map/ppermute | solution.py:252
  95.7 5.4 %collective-permute-start.18 = (bf16[256,256]{1,0:T(8,128)(2,1)S(1)}, bf16[256,256]{1,0:T(8,128)(2,1)S(1)}, u32[]{:S(2)}, u32[]{:S(2)}) collective-permute-start(bf16[256,256]{1,0:T(8,128)(2,1)S(1)} %get-tuple-element.100), channel_id=1, source_target_pairs={{0,128},{64,192},{128,0},{192,64},{1,129},{65,193},{129,1},{193,65... | collective-permute-start | bytes 393224 | tf_op jit(solution)/shard_map/ppermute | solution.py:252
  96.3 6.1 %collective-permute-start.19 = (bf16[256,256]{1,0:T(8,128)(2,1)S(1)}, bf16[256,256]{1,0:T(8,128)(2,1)S(1)}, u32[]{:S(2)}, u32[]{:S(2)}) collective-permute-start(bf16[256,256]{1,0:T(8,128)(2,1)S(1)} %get-tuple-element.101), channel_id=1, source_target_pairs={{0,64},{64,128},{128,192},{192,0},{1,65},{65,129},{129,193},{193,1... | collective-permute-start | bytes 393224 | tf_op jit(solution)/shard_map/ppermute | solution.py:252
  116.9 31.8 %all-to-all-start.1 = ((f32[16,4,512]{2,1,0:T(4,128)}), f32[16,4,512]{2,1,0:T(4,128)S(1)}, u32[]{:S(2)}, u32[]{:S(2)}) async-start(f32[16,4,512]{2,1,0:T(4,128)} %reshape.53), calls=%async_computation.1 | async-start | bytes 262144 | tf_op jit(solution)/shard_map/all_to_all | solution.py:311
  127.3 4.9 %collective-permute-start.23 = (bf16[256,256]{1,0:T(8,128)(2,1)S(1)}, bf16[256,256]{1,0:T(8,128)(2,1)S(1)}, u32[]{:S(2)}, u32[]{:S(2)}) collective-permute-start(bf16[256,256]{1,0:T(8,128)(2,1)S(1)} %get-tuple-element.109), channel_id=1, source_target_pairs={{0,16},{16,0},{32,48},{48,32},{1,17},{17,1},{33,49},{49,33},{2,18}... | collective-permute-start | bytes 393224 | tf_op jit(solution)/shard_map/ppermute | solution.py:264
  134.7 7.5 %collective-permute-start.24 = (bf16[64,512]{1,0:T(8,128)(2,1)}, bf16[64,512]{1,0:T(8,128)(2,1)S(1)}, u32[]{:S(2)}, u32[]{:S(2)}) collective-permute-start(bf16[64,512]{1,0:T(8,128)(2,1)} %get-tuple-element.111), channel_id=1, source_target_pairs={{0,12},{4,0},{8,4},{12,8},{1,13},{5,1},{9,5},{13,9},{2,14},{6,2},{... | collective-permute-start | bytes 196616 | tf_op jit(solution)/shard_map/ppermute | solution.py:252
  138.0 7.3 %collective-permute-start.25 = (bf16[64,512]{1,0:T(8,128)(2,1)}, bf16[64,512]{1,0:T(8,128)(2,1)S(1)}, u32[]{:S(2)}, u32[]{:S(2)}) collective-permute-start(bf16[64,512]{1,0:T(8,128)(2,1)} %get-tuple-element.112), channel_id=1, source_target_pairs={{0,8},{4,12},{8,0},{12,4},{1,9},{5,13},{9,1},{13,5},{2,10},{6,14},... | collective-permute-start | bytes 196616 | tf_op jit(solution)/shard_map/ppermute | solution.py:252
  140.1 6.4 %collective-permute-start.26 = (bf16[64,512]{1,0:T(8,128)(2,1)}, bf16[64,512]{1,0:T(8,128)(2,1)S(1)}, u32[]{:S(2)}, u32[]{:S(2)}) collective-permute-start(bf16[64,512]{1,0:T(8,128)(2,1)} %get-tuple-element.113), channel_id=1, source_target_pairs={{0,4},{4,8},{8,12},{12,0},{1,5},{5,9},{9,13},{13,1},{2,6},{6,10},{... | collective-permute-start | bytes 196616 | tf_op jit(solution)/shard_map/ppermute | solution.py:252
  (45 other events, 393.2 us)
